TPU v7x, 256 devices: a whole 4x4x8 slice. The times are simulated.
256 devices in a mesh: rep: 8 (over z), row: 2 (over y_lo), col: 16 (over x, y_hi, core).
Axes of the slice: x: 4, y: 4 (y_hi: 2, y_lo: 2; y = y_hi * 2 + y_lo), z: 8, core: 2. Of those that a mesh axis runs over, the one named last changes fastest.
Arguments:
- inputs: bfloat16 [8, 768, 6144], P('rep', 'col', 'row'), may hold values from -6 to 6
- pre_act: bfloat16 [8, 768, 12288], P('rep', 'row', 'col'), may hold values from -6 to 6
- out_grad: bfloat16 [8, 768, 6144], P('rep', 'col', 'row'), may hold values from -6 to 6
- w_down: bfloat16 [8, 12288, 6144], P('rep', 'col', 'row'), may hold values from -0.0546875 to 0.0546875
- q_up: bfloat16 [12288, 64], P('col'), may hold values from -6 to 6
- q_down: bfloat16 [6144, 64], P('row'), may hold values from -6 to 6
Outputs:
- p_up_out: float32 [6144, 64], P('row')
- q_up_out: float32 [12288, 64], P('col')
- p_down_out: float32 [12288, 64], P('col')
- q_down_out: float32 [6144, 64], P('row')
All inputs are finite; a program needn't handle non-finite values.
Results may differ from a plain program's by a relative error of at most 0.005.
Values may be sent and summed in bfloat16 or wider, within the bound.
No kernel may reach another device: no remote copies, remote signals or barrier semaphores. Data moves between devices by JAX's collectives and lax.ppermute only.
A program may use at most 128 MiB of HBM per device.

v0:
```python
import math

import jax
import jax.numpy as jnp
from jax import lax
from jax.sharding import PartitionSpec as P

D = 6144
FF = 12288


def gelu_value(v):
    return 0.5 * v * (1.0 + lax.erf(v / math.sqrt(2.0)))


def gelu_slope(v):
    return 0.5 * (1.0 + lax.erf(v / math.sqrt(2.0))) + v * jnp.exp(-0.5 * v * v) / math.sqrt(
        2.0 * math.pi
    )


def contract_rows(left, right):
    return lax.dot_general(
        left, right, (((0,), (0,)), ((), ())), preferred_element_type=jnp.float32
    )


def local_gram(factor):
    return jnp.dot(
        factor.T, factor, precision=lax.Precision.HIGHEST, preferred_element_type=jnp.float32
    )


def finish(factor, gram):
    lower = jnp.linalg.cholesky(gram)
    return lax.linalg.triangular_solve(lower, factor, left_side=False, lower=True, transpose_a=True)


def per_device(inputs, pre_act, out_grad, w_down, q_up, q_down):
    groups = lax.axis_size("rep")
    rows_all, grads_all = (
        lax.all_gather(inputs[0], "col", axis=0, tiled=True),
        lax.all_gather(out_grad[0], "col", axis=0, tiled=True),
    )
    scale = 1.0 / math.sqrt(rows_all.shape[0])
    weights = w_down[0]
    partial_dact = lax.dot_general(
        grads_all, weights, (((1,), (1,)), ((), ())), preferred_element_type=jnp.float32
    )
    pre_all = lax.all_gather(pre_act[0], "row", axis=0, tiled=True).astype(jnp.float32)
    act = gelu_value(pre_all).astype(jnp.bfloat16)
    dact = lax.psum(partial_dact, "row")
    dpre = (dact * gelu_slope(pre_all)).astype(jnp.bfloat16)
    grad_down = (contract_rows(act, grads_all) * scale).astype(jnp.bfloat16)
    grad_up = (contract_rows(rows_all, dpre) * scale).astype(jnp.bfloat16)
    part_up = jnp.dot(grad_up, q_up, preferred_element_type=jnp.float32)
    part_down = jnp.dot(grad_down, q_down, preferred_element_type=jnp.float32)
    p_up = lax.psum(part_up, ("rep", "col"))
    p_down = lax.psum(part_down, ("rep", "row"))
    p_up = p_up / groups
    p_down = p_down / groups
    gram_up = lax.psum(local_gram(p_up), "row")
    gram_down = lax.psum(local_gram(p_down), "col")
    hat_up = finish(p_up, gram_up)
    hat_down = finish(p_down, gram_down)
    term_up = contract_rows(grad_up, hat_up.astype(jnp.bfloat16))
    term_down = contract_rows(grad_down, hat_down.astype(jnp.bfloat16))
    q_up_new = lax.psum(term_up, ("rep", "row"))
    q_down_new = lax.psum(term_down, ("rep", "col"))
    return (hat_up * math.sqrt(D), q_up_new / groups, hat_down * math.sqrt(FF), q_down_new / groups)


def solution(mesh):
    placed = (
        P("rep", "col", "row"),
        P("rep", "row", "col"),
        P("rep", "col", "row"),
        P("rep", "col", "row"),
        P("col", None),
        P("row", None),
    )
    return jax.shard_map(
        per_device,
        mesh=mesh,
        in_specs=placed,
        out_specs=(P("row", None), P("col", None), P("col", None), P("row", None)),
        check_vma=False,
    )
```

profile of v0, /device:TPU:2, one launch (start us, length us, event | category | flops | bytes accessed | tf_op | source)
XLA Modules:
  0.0 1808.7 jit_solution(3819142777438535830)
XLA Ops:
  7.2 0.0 copy-start
  7.2 0.0 all-gather.9.cloned.1.call-start
  7.2 0.7 all-gather.9.cloned.1.call-update
  7.9 0.0 all-gather.7.cloned.1.call-start
  8.0 0.7 all-gather.7.cloned.1.call-update
  8.7 0.0 all-reduce.10.cloned.1.call-start
  8.7 32.0 %all-gather.9.cloned.1.call-done = bf16[1,768,768]{2,1,0:T(8,128)(2,1)} async-done(((bf16[1,384,768]{2,1,0:T(8,128)(2,1)}), bf16[1,768,768]{2,1,0:T(8,128)(2,1)}) %all-gather.9.cloned.1.call-update) | async-done | bytes 1179664 | tf_op jit(solution)/shard_map/all_gather | solution.py:50
  40.7 66.5 %all-gather.7.cloned.1.call-done = bf16[1,768,3072]{2,1,0:T(8,128)(2,1)} async-done(((bf16[1,48,3072]{2,1,0:T(8,128)(2,1)}), bf16[1,768,3072]{2,1,0:T(8,128)(2,1)}) %all-gather.7.cloned.1.call-update) | async-done | bytes 4718608 | tf_op jit(solution)/shard_map/all_gather | solution.py:43
  107.2 6.6 multiply_convert_fusion
  113.8 2.1 copy-done.1
  116.0 2.2 fusion.54
  118.2 0.0 all-reduce.10.cloned.1.call-update
  118.2 0.0 all-gather.11.cloned.1.call-start
  118.3 0.5 all-gather.11.cloned.1.call-update
  118.8 0.0 all-reduce.6.cloned.1.call-start
  118.8 9.0 fusion.1
  127.9 0.0 all-reduce.6.cloned.1.call-update
  127.9 0.0 all-reduce.12.cloned.1.call-start
  127.9 123.6 %all-reduce.10.cloned.1.call-done = f32[768,64]{0,1:T(8,128)} async-done(((f32[768,64]{0,1:T(8,128)}), f32[768,64]{0,1:T(8,128)}) %all-reduce.10.cloned.1.call-update) | async-done | bytes 196624 | tf_op jit(solution)/shard_map/psum | solution.py:59
  251.5 1.3 fusion.32
  252.9 57.3 %psum.54 = f32[64,64]{0,1:T(8,128)S(1)} all-reduce(f32[64,64]{0,1:T(8,128)S(1)} %fusion.32), channel_id=1, replica_groups=mesh['rep'=8,'row'=2,'col'=16] {'col'}, use_global_device_ids=true, to_apply=%region_7.9 | all-reduce | flops 4096 | bytes 32768 | tf_op jit(solution)/shard_map/psum | solution.py:63
  310.2 0.1 copy.13
  310.3 5.8 cholesky.55
  316.2 0.6 compare_reduce_fusion
  316.8 0.7 fusion.39
  317.5 4.9 custom-call.9
  322.4 2.0 broadcast_multiply_fusion.2
  324.4 4.3 fusion.34
  328.6 69.6 %all-reduce.6.cloned.1.call-done = f32[768,768]{1,0:T(8,128)} async-done(((f32[768,768]{1,0:T(8,128)}), f32[768,768]{1,0:T(8,128)}) %all-reduce.6.cloned.1.call-update) | async-done | bytes 2359312 | tf_op jit(solution)/shard_map/psum | solution.py:52
  398.2 7.6 multiply_convert_fusion.1
  405.9 2.1 copy-done.2
  408.0 1.9 fusion.55
  409.8 0.0 all-reduce.12.cloned.1.call-update
  409.8 0.0 all-reduce.8.cloned.1.call-start
  409.9 1221.8 %all-reduce.12.cloned.1.call-done = (f32[3072,64]{0,1:T(8,128)}, f32[3072,64]{0,1:T(8,128)}) async-done(((f32[3072,64]{0,1:T(8,128)}, f32[3072,64]{0,1:T(8,128)}), (f32[3072,64]{0,1:T(8,128)}, f32[3072,64]{0,1:T(8,128)})) %all-reduce.12.cloned.1.call-update) | async-done | bytes 1572880 | tf_op jit(solution)/shard_map/psum | solution.py:58
  1631.7 2.3 fusion.24
  1634.0 8.3 psum.51
  1642.3 0.1 copy.11
  1642.4 5.8 cholesky.44
  1648.3 0.6 compare_reduce_fusion.1
  1648.9 0.7 fusion.38
  1649.6 4.9 custom-call.8
  1654.5 2.9 broadcast_multiply_fusion
  1657.3 4.6 fusion.26
  1662.0 0.0 all-reduce.8.cloned.1.call-update
  1662.0 0.9 broadcast_multiply_fusion.1
  1663.0 137.2 %all-reduce.8.cloned.1.call-done = f32[768,64]{0,1:T(8,128)} async-done(((f32[768,64]{0,1:T(8,128)}), f32[768,64]{0,1:T(8,128)}) %all-reduce.8.cloned.1.call-update) | async-done | bytes 196624 | tf_op jit(solution)/shard_map/psum | solution.py:68
  1800.2 1.6 broadcast_multiply_fusion.3
  (14 shorter events, 0.1 us)
Async XLA Ops:
  7.2 108.8 %copy-start = (bf16[3072,64]{0,1:T(8,128)(2,1)S(1)}, bf16[3072,64]{0,1:T(8,128)(2,1)}, u32[]{:S(2)}) copy-start(bf16[3072,64]{0,1:T(8,128)(2,1)} %param.12) | copy-start | bytes 1179652
  7.2 33.5 %all-gather.9.cloned.1.call-start = ((), (), s32[]{:S(2)}) async-start(), calls=%async_computation.4 | async-start | bytes 1769472 | tf_op jit(solution)/shard_map/all_gather | solution.py:50
  7.9 99.2 %all-gather.7.cloned.1.call-start = ((), (), s32[]{:S(2)}) async-start(), calls=%async_computation.3 | async-start | bytes 5013504 | tf_op jit(solution)/shard_map/all_gather | solution.py:43
  8.7 242.9 %all-reduce.10.cloned.1.call-start = ((), (), s32[]{:S(2)}) async-start(), calls=%async_computation.2 | async-start | bytes 393216 | tf_op jit(solution)/shard_map/psum | solution.py:59
  113.8 2.2 copy-start.1
  118.2 210.4 %all-gather.11.cloned.1.call-start = ((), (), s32[]{:S(2)}) async-start(), calls=%async_computation.5 | async-start | bytes 5013504 | tf_op jit(solution)/shard_map/all_gather | solution.py:42
  118.8 279.4 %all-reduce.6.cloned.1.call-start = ((), (), s32[]{:S(2)}) async-start(), calls=%async_computation | async-start | bytes 4718592 | tf_op jit(solution)/shard_map/psum | solution.py:52
  127.9 1503.8 %all-reduce.12.cloned.1.call-start = ((), (), s32[]{:S(2)}) async-start(), calls=%async_computation.6 | async-start | bytes 3145728 | tf_op jit(solution)/shard_map/psum | solution.py:58
  324.4 73.8 %copy-start.5 = (bf16[1,768,768]{2,1,0:T(8,128)(2,1)S(1)}, bf16[1,768,768]{2,1,0:T(8,128)(2,1)}, u32[]{:S(2)}) copy-start(bf16[1,768,768]{2,1,0:T(8,128)(2,1)} %all-gather.9.cloned.1.call-done) | copy-start | bytes 3538948
  328.6 79.3 %copy-start.4 = (bf16[768,64]{0,1:T(8,128)(2,1)S(1)}, bf16[768,64]{0,1:T(8,128)(2,1)}, u32[]{:S(2)}) copy-start(bf16[768,64]{0,1:T(8,128)(2,1)} %param.11) | copy-start | bytes 294916
  405.8 2.1 copy-start.2
  409.8 1390.4 %all-reduce.8.cloned.1.call-start = ((), (), s32[]{:S(2)}) async-start(), calls=%async_computation.1 | async-start | bytes 393216 | tf_op jit(solution)/shard_map/psum | solution.py:68
  1657.3 4.7 copy-start.3
Sparse Core Ops, SparseCore 0:
  9.8 30.8 all-gather.8
  43.4 63.7 all-gather.6
  118.3 133.1 all-reduce.9
  254.4 61.5 all-gather.10
  318.6 79.5 all-reduce.5
  410.0 1221.6 all-reduce.11
  1662.1 138.0 all-reduce.7
where the time goes:
time: 1810 us
  waiting for transfers between devices  1650 us (91%)
  blocking collectives  65.6 us (4%)
  matrix products  44.8 us (2%)
  other arithmetic  26.7 us (1%)
    psum x1, waiting for transfers between devices, per_device(): p_up = lax.psum(part_up, ('rep', 'col'))  1220 us
    psum x1, waiting for transfers between devices, per_device(): q_up_new = lax.psum(term_up, ('rep', 'row'))  137 us
    psum x1, waiting for transfers between devices, per_device(): p_down = lax.psum(part_down, ('rep', 'row'))  124 us
    psum x1, waiting for transfers between devices, per_device(): dact = lax.psum(partial_dact, 'row')  69.6 us
    all_gather x1, waiting for transfers between devices, per_device(): lax.all_gather(out_grad[0], 'col', axis=0, tiled=True)  66.5 us
    psum x1, blocking collectives, per_device(): gram_down = lax.psum(local_gram(p_down), 'col')  57.3 us
  transfers between devices with their start and end apart: 7, of which 6 were waited for; matrix products, arithmetic and copies ran while one was open for 2% of the time, Pallas kernels for 0%

commit v1 on v0

v1 whole, which is shorter than its diff:
```python
import math

import jax
import jax.numpy as jnp
from jax import lax
from jax.experimental import pallas as pl
from jax.experimental.pallas import tpu as pltpu
from jax.sharding import PartitionSpec as P

D = 6144
FF = 12288
RANK = 64
COLS = 16
F32 = jnp.float32
BF16 = jnp.bfloat16

CORE = [(i, i ^ 1) for i in range(COLS)]
YHI = [(i, i ^ 2) for i in range(COLS)]
X_UP = [(i, (i + 4) % COLS) for i in range(COLS)]
X_DOWN = [(i, (i + 12) % COLS) for i in range(COLS)]
ROW = [(0, 1), (1, 0)]


def gather_col(own, place):
    across = lax.ppermute(own, "col", YHI)
    prev = lax.ppermute(own, "col", X_UP)
    succ = lax.ppermute(own, "col", X_DOWN)
    up = lax.ppermute(jnp.concatenate([prev[:32], across], axis=0), "col", X_UP)
    down = lax.ppermute(jnp.concatenate([succ[32:], across], axis=0), "col", X_DOWN)
    last_up = lax.ppermute(up[32:48], "col", X_UP)
    last_down = lax.ppermute(down[32:64], "col", X_DOWN)
    parts = [own, prev, succ, across, up, down, last_up, last_down]
    parts += [lax.ppermute(part, "col", CORE) for part in parts]
    return assemble(place, parts), across


PIECES = [
    [(0, 48, (0, 0), 0)],
    [(0, 48, (-1, 0), 0)],
    [(0, 48, (1, 0), 0)],
    [(0, 48, (0, 1), 0)],
    [(0, 32, (2, 0), 0), (32, 48, (-1, 1), 0)],
    [(0, 16, (2, 0), 32), (16, 48, (1, 1), 0)],
    [(0, 16, (2, 1), 0)],
    [(0, 32, (2, 1), 16)],
]
MOVES = [
    (8 * core + part, first, rows, spot, core, within)
    for core in (0, 1)
    for part, pieces in enumerate(PIECES)
    for first, rows, spot, within in pieces
]
SPOTS = sorted({(move[3], move[4]) for move in MOVES})


def assemble_kernel(place_ref, *refs):
    parts, whole = refs[:16], refs[16]
    for part, first, rows, spot, core, within in MOVES:
        start = place_ref[SPOTS.index((spot, core))] * 48 + within
        whole[pl.ds(pl.multiple_of(start, 16), rows), :] = parts[part][first : first + rows, :]


def assemble(place, parts):
    vmem = pl.BlockSpec(memory_space=pltpu.VMEM)
    return pl.pallas_call(
        assemble_kernel,
        in_specs=[pl.BlockSpec(memory_space=pltpu.SMEM)] + [vmem] * 16,
        out_specs=vmem,
        out_shape=jax.ShapeDtypeStruct((768, parts[0].shape[1]), BF16),
        compiler_params=pltpu.CompilerParams(vmem_limit_bytes=24 * 2**20),
    )(place, *parts)


def inverse_kernel(gram_ref, out_ref):
    shape = (RANK, 2 * RANK)
    i = lax.broadcasted_iota(jnp.int32, shape, 0)
    j = lax.broadcasted_iota(jnp.int32, shape, 1)
    both = jnp.concatenate([gram_ref[...], jnp.zeros((RANK, RANK), F32)], axis=1)
    both = jnp.where(j == i + RANK, 1.0, both)
    diagonal = jnp.ones((RANK, 1), F32)
    sub = lax.broadcasted_iota(jnp.int32, (RANK, 1), 0)
    for k in range(RANK):
        column = both[:, k : k + 1]
        pivot = both[k : k + 1, k : k + 1]
        diagonal = jnp.where(sub == k, pivot, diagonal)
        factor = jnp.where(sub > k, column / pivot, 0.0)
        both = both - factor * both[k : k + 1, :]
    out_ref[...] = (both / jnp.sqrt(diagonal))[:, RANK:]


def inverse_factor(gram):
    return pl.pallas_call(
        inverse_kernel, out_shape=jax.ShapeDtypeStruct((RANK, RANK), F32)
    )(gram)


def gelu_kernel(place_ref, pre_ref, act_ref, slope_ref):
    v = pre_ref[0].astype(F32)
    phi = 0.5 * (1.0 + lax.erf(v * (1.0 / math.sqrt(2.0))))
    act_ref[0] = (v * phi).astype(BF16)
    slope_ref[0] = phi + v * jnp.exp(-0.5 * v * v) * (1.0 / math.sqrt(2.0 * math.pi))


def gelu_blocks(place, pre):
    blocks, rows, cols = pre.shape
    moved = pl.BlockSpec((1, rows, cols), lambda i, place: (place[i], 0, 0))
    here = pl.BlockSpec((1, rows, cols), lambda i, place: (i, 0, 0))
    return pl.pallas_call(
        gelu_kernel,
        grid_spec=pltpu.PrefetchScalarGridSpec(
            num_scalar_prefetch=1, grid=(blocks,), in_specs=[moved], out_specs=[here, here]
        ),
        out_shape=[
            jax.ShapeDtypeStruct(pre.shape, BF16),
            jax.ShapeDtypeStruct(pre.shape, F32),
        ],
    )(place, pre)


def nn(a, b):
    return lax.dot_general(a, b, (((1,), (0,)), ((), ())), preferred_element_type=F32)


def nt(a, b):
    return lax.dot_general(a, b, (((1,), (1,)), ((), ())), preferred_element_type=F32)


def split(a):
    high = lax.reduce_precision(a, 8, 7)
    return jnp.concatenate([high.astype(BF16), (a - high).astype(BF16)], axis=0)


def fold(a):
    return a[:RANK] + a[RANK:]


def exact(a, b, dims):
    return lax.dot_general(
        a, b, (dims, ((), ())), precision=lax.Precision.HIGHEST, preferred_element_type=F32
    )


def exchange(pieces, axes):
    return lax.all_to_all(pieces, axes, 0, 0, tiled=True)


def spread(piece, axes, count):
    return exchange(jnp.broadcast_to(piece[None], (count,) + piece.shape), axes)


def pack(a):
    wide = a.shape[1] // 2
    return jnp.concatenate([a[:, :wide], a[:, wide:]], axis=0).reshape(16, 8, wide)


def unpack(a):
    a = a.reshape(2 * RANK, a.shape[-1])
    return jnp.concatenate([a[:RANK], a[RANK:]], axis=1)


def sum_rep_row(part):
    mine = exchange(pack(part), ("rep", "row")).sum(axis=0)
    return unpack(spread(mine, ("rep", "row"), 16))


def pick(flag, a, b):
    return jnp.where(flag, a, b), jnp.where(flag, b, a)


def per_device(inputs, pre_act, out_grad, w_down, q_up, q_down):
    groups = 8
    scale = 1.0 / (math.sqrt(768.0) * groups)
    row = lax.axis_index("row")
    col = lax.axis_index("col")
    x, y_hi, core = col // 4, (col // 2) % 2, col % 2
    place = jnp.stack(
        [((x + dx) % 4) * 4 + (y_hi ^ dy) * 2 + (core ^ dc) for (dx, dy), dc in SPOTS]
    ).astype(jnp.int32)

    grads, arrived = gather_col(out_grad[0], place)
    rows = lax.all_gather(inputs[0], "col", axis=0, tiled=True)

    u = nn(out_grad[0], q_down)
    high = lax.reduce_precision(u, 8, 7)
    u = jnp.concatenate([high.astype(BF16), (u - high).astype(BF16)], axis=1)
    u = spread(u, ("row", "col"), 32).reshape(2, 768, 2 * RANK)
    u = lax.dynamic_slice(u, (0, row * 384, 0), (2, 384, 2 * RANK))
    u = jnp.concatenate([u[0], u[1]], axis=1)
    own = pre_act[0].astype(F32)
    act_own = (0.5 * own * (1.0 + lax.erf(own * (1.0 / math.sqrt(2.0))))).astype(BF16)
    p_down = lax.dot_general(u, act_own, (((0,), (0,)), ((), ())), preferred_element_type=F32)
    p_down = sum_rep_row(fold(p_down[: 2 * RANK] + p_down[2 * RANK :]) * scale)
    gram_down = exact(p_down, p_down, ((1,), (1,)))
    gram_down = jnp.concatenate([gram_down[:32], gram_down[32:]], axis=1)
    gram_down = spread(gram_down, "col", 16).sum(axis=0)
    gram_down = jnp.concatenate([gram_down[:, :RANK], gram_down[:, RANK:]], axis=0)
    inverse_down = inverse_factor(gram_down)
    p_hat_down = exact(inverse_down, p_down, ((1,), (0,)))

    own_pre, _ = lax.optimization_barrier((pre_act[0], arrived))
    pre_other = lax.ppermute(own_pre, "row", ROW)
    pre_all = jnp.concatenate([own_pre, pre_other], axis=0).reshape(16, 48, 768)
    act, slope = gelu_blocks(jnp.arange(16, dtype=jnp.int32) ^ (row * 8), pre_all)
    act = act.reshape(768, 768)
    slope = slope.reshape(768, 768)

    dact = nt(grads, w_down[0])
    dpre = (dact * slope).astype(BF16)
    z_part = nt(q_up.T, dpre)
    z = z_part + lax.ppermute(z_part, "row", ROW)

    s = nt(p_hat_down.astype(BF16), act)
    q_part = fold(nn(split(s), grads))
    p_part = fold(nn(split(z), rows)) * scale
    first = core == 0
    mine, other = pick(first, p_part, q_part)
    mine = mine + lax.ppermute(other.astype(BF16), "col", CORE).astype(F32)
    chips = [[2 * i + k for i in range(8)] for k in (0, 1)]
    mine = lax.all_to_all(
        mine.astype(BF16).reshape(8, 8, 3072), "col", 0, 0, tiled=True, axis_index_groups=chips
    )
    mine = mine.astype(F32).sum(axis=0).astype(BF16)
    mine = spread(mine, "rep", 8).astype(F32).sum(axis=0).astype(BF16)
    mine = lax.all_to_all(
        jnp.broadcast_to(mine[None], (8, 8, 3072)), "col", 0, 0, tiled=True, axis_index_groups=chips
    ).reshape(RANK, 3072)
    p_up, q_down_raw = pick(first, mine, lax.ppermute(mine, "col", CORE))

    w_part = nt(p_up, rows)
    w = w_part + lax.ppermute(w_part, "row", ROW)
    y = sum_rep_row(fold(nn(split(w), dpre)))

    p_up = p_up.astype(F32)
    gram_up = exact(p_up, p_up, ((1,), (1,)))
    gram_up = gram_up + lax.ppermute(gram_up, "row", ROW)
    inverse_up = inverse_factor(gram_up)
    dims = ((1,), (0,))
    p_up_out = exact(inverse_up * math.sqrt(D), p_up, dims)
    q_up_out = exact(inverse_up * scale, y, dims)
    p_down_out = p_hat_down * math.sqrt(FF)
    q_down_out = q_down_raw.astype(F32) * scale
    return p_up_out.T, q_up_out.T, p_down_out.T, q_down_out.T


def solution(mesh):
    placed = (
        P("rep", "col", "row"),
        P("rep", "row", "col"),
        P("rep", "col", "row"),
        P("rep", "col", "row"),
        P("col", None),
        P("row", None),
    )
    return jax.shard_map(
        per_device,
        mesh=mesh,
        in_specs=placed,
        out_specs=(P("row", None), P("col", None), P("col", None), P("row", None)),
        check_vma=False,
    )
```

time: 1810 us -> 232 us (0.13)
  waiting for transfers between devices: 1650 us -> 42.8 us
  starting transfers between devices: 0.28 us -> 50.1 us
  Pallas kernels: 0 us -> 26.1 us
  matrix products: 44.8 us -> 23 us
    psum x4 -> x0, waiting for transfers between devices: 1550 us -> none  [the longest x1 1220 us: per_device(): p_up = lax.psum(part_up, ('rep', 'col'))]
    all_gather x3 -> x1, waiting for transfers between devices: 98.4 us -> 0.01 us  [per_device(): rows = lax.all_gather(inputs[0], 'col', axis=0, tiled=True)]
    psum x2 -> x0, blocking collectives: 65.6 us -> none  [the longest x1 57.3 us: per_device(): gram_down = lax.psum(local_gram(p_down), 'col')]
    all_to_all x0 -> x3, blocking collectives: none -> 48.8 us  [the longest x1 19.6 us: exchange(): return lax.all_to_all(pieces, axes, 0, 0, tiled=True)]
    all_to_all x0 -> x6, starting transfers between devices: none -> 34.2 us  [exchange(): return lax.all_to_all(pieces, axes, 0, 0, tiled=True)]
    pallas_call x0 -> x4, Pallas kernels: none -> 26.1 us  [the longest x2 14 us: inverse_factor(): pl.pallas_call(inverse_kernel, out_shape=jax.ShapeDtypeStruct((RANK, RANK...]
    ppermute x0 -> x21, waiting for transfers between devices: none -> 24.7 us  [the longest x1 10.6 us: gather_col(): succ = lax.ppermute(own, 'col', X_DOWN)]
    another operation x10 -> x0, other arithmetic: 24.1 us -> none  [the longest x6 13 us: finish(): lower = jnp.linalg.cholesky(gram)]
  transfers between devices with their start and end apart: 7 -> 28, of which waited for: 6 -> 7; matrix products, arithmetic and copies ran while one was open for 2% -> 14% of each run, Pallas kernels for 0% -> 11%
where the time goes in v1:
time: 232 us; the launch traced here: 229 us
  starting transfers between devices  50.1 us (22%)
  blocking collectives  48.8 us (21%)
  waiting for transfers between devices  42.8 us (18%)
  Pallas kernels  26.1 us (11%)
  matrix products  23 us (10%)
  between operations  14.6 us (6%)
  other arithmetic  12.4 us (5%)
  local copies, waits for them, and re-layouts  10.7 us (5%)
    all_to_all x6, starting transfers between devices, exchange(): return lax.all_to_all(pieces, axes, 0, 0, tiled=True)  34.2 us
    all_to_all x1, blocking collectives, exchange(): return lax.all_to_all(pieces, axes, 0, 0, tiled=True)  19.6 us
    all_to_all x6, waiting for transfers between devices, exchange(): return lax.all_to_all(pieces, axes, 0, 0, tiled=True)  17.4 us
    all_to_all x1, blocking collectives, per_device(): lax.all_to_all(mine.astype(BF16).reshape(8, 8, 3072), 'col', 0, 0, tiled=...  16.4 us
    pallas_call x2, Pallas kernels, inverse_factor(): pl.pallas_call(inverse_kernel, out_shape=jax.ShapeDtypeStruct((RANK, RANK...  14 us
    all_to_all x1, blocking collectives, per_device(): lax.all_to_all(jnp.broadcast_to(mine[None], (8, 8, 3072)), 'col', 0, 0, t...  12.8 us
    ppermute x1, waiting for transfers between devices, gather_col(): succ = lax.ppermute(own, 'col', X_DOWN)  10.6 us
    pallas_call x1, Pallas kernels, gelu_blocks(): pl.pallas_call(gelu_kernel, grid_spec=pltpu.PrefetchScalarGridSpec(num_sc...  10.4 us
  transfers between devices with their start and end apart: 28, of which 7 were waited for; matrix products, arithmetic and copies ran while one was open for 14% of the time, Pallas kernels for 11%

profile of v1, /device:TPU:2, one launch (start us, length us, event | category | flops | bytes accessed | tf_op | source)
XLA Modules:
  0.0 228.5 jit_solution(14140265173236580447)
XLA Ops:
  7.9 3.3 %collective-permute-start.2 = (bf16[48,3072]{1,0:T(8,128)(2,1)}, bf16[48,3072]{1,0:T(8,128)(2,1)S(1)}, u32[]{:S(2)}, u32[]{:S(2)}) collective-permute-start(bf16[48,3072]{1,0:T(8,128)(2,1)} %bitcast.82), channel_id=1, source_target_pairs={{0,2},{1,3},{2,0},{3,1},{4,6},{5,7},{6,4},{7,5},{8,10},{9,11},{10,... | collective-permute-start | bytes 884744 | tf_op jit(solution)/shard_map/ppermute | solution.py:25
  11.2 1.5 collective-permute-start
  12.7 1.2 reduce-precision_convert_fusion.3
  14.0 0.8 broadcast_in_dim.12
  14.8 5.2 %all-to-all-start = ((bf16[32,48,128]{2,1,0:T(8,128)(2,1)}), bf16[32,48,128]{2,1,0:T(8,128)(2,1)S(1)}, u32[]{:S(2)}, u32[]{:S(2)}) async-start(bf16[32,48,128]{2,1,0:T(8,128)(2,1)} %broadcast_in_dim.12), calls=%async_computation | async-start | bytes 786432 | tf_op jit(solution)/shard_map/all_to_all | solution.py:144
  20.4 0.8 pad_maximum_fusion.1
  21.2 1.8 collective-permute-start.3
  23.0 1.5 collective-permute-start.15
  24.5 10.6 %collective-permute-done.1.refs_2_ = bf16[48,3072]{1,0:T(8,128)(2,1)S(1)} collective-permute-done((bf16[48,3072]{1,0:T(8,128)(2,1)S(1)}, bf16[48,3072]{1,0:T(8,128)(2,1)S(1)}, u32[]{:S(2)}, u32[]{:S(2)}) %collective-permute-start.1) | collective-permute-done | bytes 294944 | tf_op jit(solution)/shard_map/ppermute | solution.py:27
  35.2 1.5 fusion.14
  37.5 10.3 %all-to-all-start.1 = ((f32[16,8,384]{2,1,0:T(8,128)}), f32[16,8,384]{2,1,0:T(8,128)S(1)}, u32[]{:S(2)}, u32[]{:S(2)}) async-start(f32[16,8,384]{2,1,0:T(8,128)} %maximum_bitcast_fusion), calls=%async_computation.1 | async-start | bytes 393216 | tf_op jit(solution)/shard_map/all_to_all | solution.py:144
  47.8 0.8 pad_maximum_fusion.2
  49.1 9.6 %all-to-all-done.1 = f32[16,8,384]{2,1,0:T(8,128)S(1)} async-done(((f32[16,8,384]{2,1,0:T(8,128)}), f32[16,8,384]{2,1,0:T(8,128)S(1)}, u32[]{:S(2)}, u32[]{:S(2)}) %all-to-all-start.1) | async-done | bytes 196640 | tf_op jit(solution)/shard_map/all_to_all | solution.py:144
  59.4 4.2 %all-to-all-start.2 = ((f32[16,8,384]{2,1,0:T(8,128)}), f32[16,8,384]{2,1,0:T(8,128)}, u32[]{:S(2)}, u32[]{:S(2)}) async-start(f32[16,8,384]{2,1,0:T(8,128)} %broadcast_in_dim.13), calls=%async_computation.2 | async-start | bytes 393216 | tf_op jit(solution)/shard_map/all_to_all | solution.py:144
  66.7 2.4 %pad_maximum_fusion = bf16[768,768]{1,0:T(8,128)(2,1)} fusion(bf16[384,768]{1,0:T(8,128)(2,1)} %collective-permute-done.15, bf16[384,768]{1,0:T(8,128)(2,1)} %bitcast.18), kind=kLoop, calls=%fused_computation.14 | loop fusion | flops 2359296 | bytes 2359296 | tf_op jit(solution)/shard_map/concatenate | solution.py:202
  69.1 10.4 %shard_map.94 = (bf16[16,48,768]{2,1,0:T(8,128)(2,1)}, f32[16,48,768]{2,1,0:T(8,128)}) custom-call(s32[16]{0:T(128)} %iota_xor_fusion.place_ref, bf16[16,48,768]{2,1,0:T(8,128)(2,1)} %bitcast.87), custom_call_target="tpu_custom_call" | custom-call | tf_op jit(solution)/shard_map/pallas_call | solution.py:108
  79.6 1.0 slice_bitcast_fusion.3
  80.6 0.7 copy-done.3
  82.2 1.8 collective-permute-start.5
  84.2 3.7 %collective-permute-done.5.refs_6_ = bf16[16,3072]{1,0:T(8,128)(2,1)} collective-permute-done((bf16[16,3072]{1,0:T(8,128)(2,1)}, bf16[16,3072]{1,0:T(8,128)(2,1)}, u32[]{:S(2)}, u32[]{:S(2)}) %collective-permute-start.5) | collective-permute-done | bytes 98336 | tf_op jit(solution)/shard_map/ppermute | solution.py:30
  88.7 7.4 %all-to-all-start.3 = ((f32[16,32,128]{2,1,0:T(8,128)}), f32[16,32,128]{2,1,0:T(8,128)}, u32[]{:S(2)}, u32[]{:S(2)}) async-start(f32[16,32,128]{2,1,0:T(8,128)} %broadcast_in_dim.14), calls=%async_computation.3 | async-start | bytes 524288 | tf_op jit(solution)/shard_map/all_to_all | solution.py:144
  96.1 1.0 copy-done.4
  97.1 1.7 shard_map.93
  98.8 1.1 copy-done.12
  99.9 2.4 %copy-done.13 = f32[16,48,768]{2,1,0:T(8,128)S(1)} copy-done((f32[16,48,768]{2,1,0:T(8,128)S(1)}, f32[16,48,768]{2,1,0:T(8,128)}, u32[]{:S(2)}) %copy-start.13) | copy-done | bytes 2359320
  102.3 3.9 %fusion.6 = bf16[768,768]{1,0:T(8,128)(2,1)S(1)} fusion(f32[16,48,768]{2,1,0:T(8,128)S(1)} %copy-done.13, bf16[768,3072]{1,0:T(8,128)(2,1)S(1)} %shard_map.93, bf16[1,768,3072]{2,1,0:T(8,128)(2,1)S(1)} %copy-done.12), kind=kOutput, calls=%fused_computation.7 | convolution fusion | flops 3625058304 | bytes 12976128 | tf_op jit(solution)/shard_map/dot_general | solution.py:125
  106.7 1.2 collective-permute-start.16
  107.9 1.0 reduce_sum.52
  109.6 7.0 %shard_map.95 = f32[64,64]{1,0:T(8,128)} custom-call(f32[64,64]{1,0:T(8,128)} %pad_maximum_fusion.6.gram_ref), custom_call_target="tpu_custom_call" | custom-call | tf_op jit(solution)/shard_map/pallas_call | solution.py:92
  116.6 1.1 fusion.39
  118.2 3.1 %fusion.27 = f32[128,3072]{1,0:T(8,128)S(1)} fusion(bf16[768,3072]{1,0:T(8,128)(2,1)} %copy-done.1, bf16[64,768]{1,0:T(8,128)(2,1)S(1)} %get-tuple-element.21, bf16[64,768]{1,0:T(8,128)(2,1)S(1)} %get-tuple-element.20), kind=kOutput, calls=%fused_computation.48 | convolution fusion | flops 604372992 | bytes 6488064 | tf_op jit(solution)/shard_map/dot_general | solution.py:121
  121.3 1.6 reduce-precision_convert_fusion.2
  123.0 3.2 %fusion.2 = f32[128,3072]{1,0:T(8,128)S(1)} fusion(bf16[1,768,3072]{2,1,0:T(8,128)(2,1)} %all-gather.3.cloned.1.call-done, bf16[64,768]{1,0:T(8,128)(2,1)} %get-tuple-element.13, bf16[64,768]{1,0:T(8,128)(2,1)} %get-tuple-element.12), kind=kOutput, calls=%fused_computation.2 | convolution fusion | flops 604372992 | bytes 6488064 | tf_op jit(solution)/shard_map/dot_general | solution.py:121
  126.5 1.7 collective-permute-done.17
  128.5 16.4 %all_to_all.45 = bf16[8,8,3072]{2,1,0:T(8,128)(2,1)S(1)} all-to-all(bf16[8,8,3072]{2,1,0:T(8,128)(2,1)S(1)} %fusion.16), channel_id=1, replica_groups={{0,2,4,6,8,10,12,14},{1,3,5,7,9,11,13,15},{16,18,20,22,24,26,28,30},{17..., dimensions={0} | all-to-all | bytes 786432 | tf_op jit(solution)/shard_map/all_to_all | solution.py:219
  145.0 19.6 %all_to_all.46 = bf16[8,8,3072]{2,1,0:T(8,128)(2,1)S(1)} all-to-all(bf16[8,8,3072]{2,1,0:T(8,128)(2,1)S(1)} %broadcast_in_dim.15), channel_id=1, replica_groups=mesh['rep'=8,'row'=2,'col'=16] {'rep'}, dimensions={0} | all-to-all | bytes 786432 | tf_op jit(solution)/shard_map/all_to_all | solution.py:144
  164.7 12.8 %all_to_all.47 = bf16[8,8,3072]{2,1,0:T(8,128)(2,1)S(1)} all-to-all(bf16[8,8,3072]{2,1,0:T(8,128)(2,1)S(1)} %broadcast_in_dim.16), channel_id=1, replica_groups={{0,2,4,6,8,10,12,14},{1,3,5,7,9,11,13,15},{16,18,20,22,24,26,28,30},{17..., dimensions={0} | all-to-all | bytes 786432 | tf_op jit(solution)/shard_map/all_to_all | solution.py:224
  177.5 1.7 collective-permute-done.18
  179.3 3.9 %fusion = f32[64,768]{1,0:T(8,128)S(1)} fusion(bf16[64,3072]{1,0:T(8,128)(2,1)S(1)} %broadcast_select_fusion, bf16[1,768,3072]{2,1,0:T(8,128)(2,1)} %all-gather.3.cloned.1.call-done), kind=kOutput, calls=%fused_computation | convolution fusion | flops 301989888 | bytes 5308416 | tf_op jit(solution)/shard_map/dot_general | solution.py:125
  183.5 6.9 %collective-permute-done.20 = f32[64,768]{1,0:T(8,128)S(1)} collective-permute-done((f32[64,768]{1,0:T(8,128)S(1)}, f32[64,768]{1,0:T(8,128)S(1)}, u32[]{:S(2)}, u32[]{:S(2)}) %collective-permute-start.20) | collective-permute-done | bytes 196640 | tf_op jit(solution)/shard_map/ppermute | solution.py:230
  191.5 3.5 %all-to-all-start.7 = ((f32[16,8,384]{2,1,0:T(8,128)}), f32[16,8,384]{2,1,0:T(8,128)S(1)}, u32[]{:S(2)}, u32[]{:S(2)}) async-start(f32[16,8,384]{2,1,0:T(8,128)} %maximum_bitcast_fusion.1), calls=%async_computation.7 | async-start | bytes 393216 | tf_op jit(solution)/shard_map/all_to_all | solution.py:144
  196.0 1.9 collective-permute-start.19
  197.9 7.8 %all-to-all-done.7 = f32[16,8,384]{2,1,0:T(8,128)S(1)} async-done(((f32[16,8,384]{2,1,0:T(8,128)}), f32[16,8,384]{2,1,0:T(8,128)S(1)}, u32[]{:S(2)}, u32[]{:S(2)}) %all-to-all-start.7) | async-done | bytes 196640 | tf_op jit(solution)/shard_map/all_to_all | solution.py:144
  206.4 3.5 %all-to-all-start.8 = ((f32[16,8,384]{2,1,0:T(8,128)}), f32[16,8,384]{2,1,0:T(8,128)S(1)}, u32[]{:S(2)}, u32[]{:S(2)}) async-start(f32[16,8,384]{2,1,0:T(8,128)} %broadcast_in_dim.17), calls=%async_computation.8 | async-start | bytes 393216 | tf_op jit(solution)/shard_map/all_to_all | solution.py:144
  209.9 1.0 multiply_bitcast_fusion
  211.5 7.0 %shard_map.96 = f32[64,64]{1,0:T(8,128)} custom-call(f32[64,64]{1,0:T(8,128)} %add.209.gram_ref), custom_call_target="tpu_custom_call" | custom-call | tf_op jit(solution)/shard_map/pallas_call | solution.py:92
  218.5 2.2 fusion.44
  220.7 1.0 fusion.35
  (101 shorter events, 14.3 us)
Async XLA Ops:
  7.2 5.5 %copy-start = (bf16[3072,64]{0,1:T(8,128)(2,1)S(1)}, bf16[3072,64]{0,1:T(8,128)(2,1)}, u32[]{:S(2)}) copy-start(bf16[3072,64]{0,1:T(8,128)(2,1)} %param.11) | copy-start | bytes 1179652
  7.2 12.9 %copy-start.2 = (bf16[1,48,3072]{2,1,0:T(8,128)(2,1)S(1)}, bf16[1,48,3072]{2,1,0:T(8,128)(2,1)}, u32[]{:S(2)}) copy-start(bf16[1,48,3072]{2,1,0:T(8,128)(2,1)} %param.8) | copy-start | bytes 884740
  7.2 115.8 %all-gather.3.cloned.1.call-start = ((), (), s32[]{:S(2)}) async-start(), calls=%async_computation.9 | async-start | bytes 5013504 | tf_op jit(solution)/shard_map/all_gather | solution.py:181
  7.9 12.5 %collective-permute-start.2 = (bf16[48,3072]{1,0:T(8,128)(2,1)}, bf16[48,3072]{1,0:T(8,128)(2,1)S(1)}, u32[]{:S(2)}, u32[]{:S(2)}) collective-permute-start(bf16[48,3072]{1,0:T(8,128)(2,1)} %bitcast.82), channel_id=1, source_target_pairs={{0,2},{1,3},{2,0},{3,1},{4,6},{5,7},{6,4},{7,5},{8,10},{9,11},{10,... | collective-permute-start | bytes 884744 | tf_op jit(solution)/shard_map/ppermute | solution.py:25
  11.2 9.2 %collective-permute-start = (bf16[48,3072]{1,0:T(8,128)(2,1)}, bf16[48,3072]{1,0:T(8,128)(2,1)S(1)}, u32[]{:S(2)}, u32[]{:S(2)}) collective-permute-start(bf16[48,3072]{1,0:T(8,128)(2,1)} %bitcast.83), channel_id=1, source_target_pairs={{0,4},{1,5},{2,6},{3,7},{4,8},{5,9},{6,10},{7,11},{8,12},{9,13},{1... | collective-permute-start | bytes 884744 | tf_op jit(solution)/shard_map/ppermute | solution.py:26
  14.8 20.3 %all-to-all-start = ((bf16[32,48,128]{2,1,0:T(8,128)(2,1)}), bf16[32,48,128]{2,1,0:T(8,128)(2,1)S(1)}, u32[]{:S(2)}, u32[]{:S(2)}) async-start(bf16[32,48,128]{2,1,0:T(8,128)(2,1)} %broadcast_in_dim.12), calls=%async_computation | async-start | bytes 786432 | tf_op jit(solution)/shard_map/all_to_all | solution.py:144
  20.1 15.1 %collective-permute-start.1 = (bf16[48,3072]{1,0:T(8,128)(2,1)S(1)}, bf16[48,3072]{1,0:T(8,128)(2,1)S(1)}, u32[]{:S(2)}, u32[]{:S(2)}) collective-permute-start(bf16[48,3072]{1,0:T(8,128)(2,1)S(1)} %bitcast.84), channel_id=1, source_target_pairs={{0,12},{1,13},{2,14},{3,15},{4,0},{5,1},{6,2},{7,3},{8,4},{9,5},{1... | collective-permute-start | bytes 884744 | tf_op jit(solution)/shard_map/ppermute | solution.py:27
  21.2 44.5 %collective-permute-start.3 = (bf16[80,3072]{1,0:T(8,128)(2,1)}, bf16[80,3072]{1,0:T(8,128)(2,1)S(1)}, u32[]{:S(2)}, u32[]{:S(2)}) collective-permute-start(bf16[80,3072]{1,0:T(8,128)(2,1)} %pad_maximum_fusion.1), channel_id=1, source_target_pairs={{0,4},{1,5},{2,6},{3,7},{4,8},{5,9},{6,10},{7,11},{8,12},{9,13},{1... | collective-permute-start | bytes 1474568 | tf_op jit(solution)/shard_map/ppermute | solution.py:28
  23.0 43.6 %collective-permute-start.15 = (bf16[384,768]{1,0:T(8,128)(2,1)}, bf16[384,768]{1,0:T(8,128)(2,1)}, u32[]{:S(2)}, u32[]{:S(2)}) collective-permute-start(bf16[384,768]{1,0:T(8,128)(2,1)} %bitcast.18), channel_id=1, source_target_pairs={{0,16},{16,0},{1,17},{17,1},{2,18},{18,2},{3,19},{19,3},{4,20},{20... | collective-permute-start | bytes 1769480 | tf_op jit(solution)/shard_map/ppermute | solution.py:201
  37.5 21.2 %all-to-all-start.1 = ((f32[16,8,384]{2,1,0:T(8,128)}), f32[16,8,384]{2,1,0:T(8,128)S(1)}, u32[]{:S(2)}, u32[]{:S(2)}) async-start(f32[16,8,384]{2,1,0:T(8,128)} %maximum_bitcast_fusion), calls=%async_computation.1 | async-start | bytes 393216 | tf_op jit(solution)/shard_map/all_to_all | solution.py:144
  48.6 16.3 %collective-permute-start.4 = (bf16[64,3072]{1,0:T(8,128)(2,1)}, bf16[64,3072]{1,0:T(8,128)(2,1)S(1)}, u32[]{:S(2)}, u32[]{:S(2)}) collective-permute-start(bf16[64,3072]{1,0:T(8,128)(2,1)} %pad_maximum_fusion.2), channel_id=1, source_target_pairs={{0,12},{1,13},{2,14},{3,15},{4,0},{5,1},{6,2},{7,3},{8,4},{9,5},{1... | collective-permute-start | bytes 1179656 | tf_op jit(solution)/shard_map/ppermute | solution.py:29
  59.4 20.1 %all-to-all-start.2 = ((f32[16,8,384]{2,1,0:T(8,128)}), f32[16,8,384]{2,1,0:T(8,128)}, u32[]{:S(2)}, u32[]{:S(2)}) async-start(f32[16,8,384]{2,1,0:T(8,128)} %broadcast_in_dim.13), calls=%async_computation.2 | async-start | bytes 393216 | tf_op jit(solution)/shard_map/all_to_all | solution.py:144
  63.6 16.9 %collective-permute-start.7 = (bf16[48,3072]{1,0:T(8,128)(2,1)S(1)}, bf16[48,3072]{1,0:T(8,128)(2,1)S(1)}, u32[]{:S(2)}, u32[]{:S(2)}) collective-permute-start(bf16[48,3072]{1,0:T(8,128)(2,1)S(1)} %bitcast.85), channel_id=1, source_target_pairs={{0,1},{1,0},{2,3},{3,2},{4,5},{5,4},{6,7},{7,6},{8,9},{9,8},{10,11... | collective-permute-start | bytes 884744 | tf_op jit(solution)/shard_map/ppermute | solution.py:33
  64.5 17.5 %collective-permute-start.10 = (bf16[48,3072]{1,0:T(8,128)(2,1)S(1)}, bf16[48,3072]{1,0:T(8,128)(2,1)}, u32[]{:S(2)}, u32[]{:S(2)}) collective-permute-start(bf16[48,3072]{1,0:T(8,128)(2,1)S(1)} %collective-permute-done.2.refs_3_), channel_id=1, source_target_pairs={{0,1},{1,0},{2,3},{3,2},{4,5},{5,4},{6,7},{7,6},{8,9},{9,8},{10,11... | collective-permute-start | bytes 884744 | tf_op jit(solution)/shard_map/ppermute | solution.py:33
  64.9 17.3 %collective-permute-start.8 = (bf16[48,3072]{1,0:T(8,128)(2,1)S(1)}, bf16[48,3072]{1,0:T(8,128)(2,1)}, u32[]{:S(2)}, u32[]{:S(2)}) collective-permute-start(bf16[48,3072]{1,0:T(8,128)(2,1)S(1)} %collective-permute-done.refs_1_), channel_id=1, source_target_pairs={{0,1},{1,0},{2,3},{3,2},{4,5},{5,4},{6,7},{7,6},{8,9},{9,8},{10,11... | collective-permute-start | bytes 884744 | tf_op jit(solution)/shard_map/ppermute | solution.py:33
  65.7 18.3 %collective-permute-start.6 = (bf16[32,3072]{1,0:T(8,128)(2,1)}, bf16[32,3072]{1,0:T(8,128)(2,1)S(1)}, u32[]{:S(2)}, u32[]{:S(2)}) collective-permute-start(bf16[32,3072]{1,0:T(8,128)(2,1)} %slice.131), channel_id=1, source_target_pairs={{0,12},{1,13},{2,14},{3,15},{4,0},{5,1},{6,2},{7,3},{8,4},{9,5},{1... | collective-permute-start | bytes 589832 | tf_op jit(solution)/shard_map/ppermute | solution.py:31
  66.6 29.5 %collective-permute-start.11 = (bf16[80,3072]{1,0:T(8,128)(2,1)S(1)}, bf16[80,3072]{1,0:T(8,128)(2,1)S(1)}, u32[]{:S(2)}, u32[]{:S(2)}) collective-permute-start(bf16[80,3072]{1,0:T(8,128)(2,1)S(1)} %collective-permute-done.3.refs_4_), channel_id=1, source_target_pairs={{0,1},{1,0},{2,3},{3,2},{4,5},{5,4},{6,7},{7,6},{8,9},{9,8},{10,11... | collective-permute-start | bytes 1474568 | tf_op jit(solution)/shard_map/ppermute | solution.py:33
  80.5 3.5 %copy-start.6 = (f32[64,384]{1,0:T(8,128)}, f32[64,384]{1,0:T(8,128)S(1)}, u32[]{:S(2)}) copy-start(f32[64,384]{1,0:T(8,128)S(1)} %get-tuple-element.22) | copy-start | bytes 294916
  80.5 3.6 %copy-start.8 = (f32[64,384]{1,0:T(8,128)}, f32[64,384]{1,0:T(8,128)S(1)}, u32[]{:S(2)}) copy-start(f32[64,384]{1,0:T(8,128)S(1)} %get-tuple-element.23) | copy-start | bytes 294916
  80.5 0.7 copy-start.3
  81.3 14.8 %collective-permute-start.12 = (bf16[64,3072]{1,0:T(8,128)(2,1)S(1)}, bf16[64,3072]{1,0:T(8,128)(2,1)S(1)}, u32[]{:S(2)}, u32[]{:S(2)}) collective-permute-start(bf16[64,3072]{1,0:T(8,128)(2,1)S(1)} %collective-permute-done.4.refs_5_), channel_id=1, source_target_pairs={{0,1},{1,0},{2,3},{3,2},{4,5},{5,4},{6,7},{7,6},{8,9},{9,8},{10,11... | collective-permute-start | bytes 1179656 | tf_op jit(solution)/shard_map/ppermute | solution.py:33
  82.0 14.1 %collective-permute-start.9 = (bf16[48,3072]{1,0:T(8,128)(2,1)S(1)}, bf16[48,3072]{1,0:T(8,128)(2,1)}, u32[]{:S(2)}, u32[]{:S(2)}) collective-permute-start(bf16[48,3072]{1,0:T(8,128)(2,1)S(1)} %collective-permute-done.1.refs_2_), channel_id=1, source_target_pairs={{0,1},{1,0},{2,3},{3,2},{4,5},{5,4},{6,7},{7,6},{8,9},{9,8},{10,11... | collective-permute-start | bytes 884744 | tf_op jit(solution)/shard_map/ppermute | solution.py:33
  82.2 5.6 %collective-permute-start.5 = (bf16[16,3072]{1,0:T(8,128)(2,1)}, bf16[16,3072]{1,0:T(8,128)(2,1)}, u32[]{:S(2)}, u32[]{:S(2)}) collective-permute-start(bf16[16,3072]{1,0:T(8,128)(2,1)} %slice.130), channel_id=1, source_target_pairs={{0,4},{1,5},{2,6},{3,7},{4,8},{5,9},{6,10},{7,11},{8,12},{9,13},{1... | collective-permute-start | bytes 294920 | tf_op jit(solution)/shard_map/ppermute | solution.py:30
  84.0 12.1 %collective-permute-start.14 = (bf16[32,3072]{1,0:T(8,128)(2,1)S(1)}, bf16[32,3072]{1,0:T(8,128)(2,1)}, u32[]{:S(2)}, u32[]{:S(2)}) collective-permute-start(bf16[32,3072]{1,0:T(8,128)(2,1)S(1)} %collective-permute-done.6.refs_7_), channel_id=1, source_target_pairs={{0,1},{1,0},{2,3},{3,2},{4,5},{5,4},{6,7},{7,6},{8,9},{9,8},{10,11... | collective-permute-start | bytes 589832 | tf_op jit(solution)/shard_map/ppermute | solution.py:33
  87.8 8.2 %collective-permute-start.13 = (bf16[16,3072]{1,0:T(8,128)(2,1)}, bf16[16,3072]{1,0:T(8,128)(2,1)}, u32[]{:S(2)}, u32[]{:S(2)}) collective-permute-start(bf16[16,3072]{1,0:T(8,128)(2,1)} %collective-permute-done.5.refs_6_), channel_id=1, source_target_pairs={{0,1},{1,0},{2,3},{3,2},{4,5},{5,4},{6,7},{7,6},{8,9},{9,8},{10,11... | collective-permute-start | bytes 294920 | tf_op jit(solution)/shard_map/ppermute | solution.py:33
  88.7 19.2 %all-to-all-start.3 = ((f32[16,32,128]{2,1,0:T(8,128)}), f32[16,32,128]{2,1,0:T(8,128)}, u32[]{:S(2)}, u32[]{:S(2)}) async-start(f32[16,32,128]{2,1,0:T(8,128)} %broadcast_in_dim.14), calls=%async_computation.3 | async-start | bytes 524288 | tf_op jit(solution)/shard_map/all_to_all | solution.py:144
  96.1 1.0 copy-start.4
  97.1 2.8 %copy-start.12 = (bf16[1,768,3072]{2,1,0:T(8,128)(2,1)S(1)}, bf16[1,768,3072]{2,1,0:T(8,128)(2,1)}, u32[]{:S(2)}) copy-start(bf16[1,768,3072]{2,1,0:T(8,128)(2,1)} %param.9) | copy-start | bytes 14155780
  97.1 5.2 %copy-start.13 = (f32[16,48,768]{2,1,0:T(8,128)S(1)}, f32[16,48,768]{2,1,0:T(8,128)}, u32[]{:S(2)}) copy-start(f32[16,48,768]{2,1,0:T(8,128)} %get-tuple-element.8) | copy-start | bytes 7077892
  98.8 7.3 %copy-start.1 = (bf16[768,3072]{1,0:T(8,128)(2,1)}, bf16[768,3072]{1,0:T(8,128)(2,1)S(1)}, u32[]{:S(2)}) copy-start(bf16[768,3072]{1,0:T(8,128)(2,1)S(1)} %shard_map.93) | copy-start | bytes 14155780
  102.3 3.9 %copy-start.11 = (bf16[768,64]{0,1:T(8,128)(2,1)S(1)}, bf16[768,64]{0,1:T(8,128)(2,1)}, u32[]{:S(2)}) copy-start(bf16[768,64]{0,1:T(8,128)(2,1)} %param.10) | copy-start | bytes 294916
  106.2 10.4 %copy-start.7 = (f32[64,384]{1,0:T(8,128)S(1)}, f32[64,384]{1,0:T(8,128)}, u32[]{:S(2)}) copy-start(f32[64,384]{1,0:T(8,128)} %copy-done.6) | copy-start | bytes 294916
  106.2 10.4 %copy-start.9 = (f32[64,384]{1,0:T(8,128)S(1)}, f32[64,384]{1,0:T(8,128)}, u32[]{:S(2)}) copy-start(f32[64,384]{1,0:T(8,128)} %copy-done.8) | copy-start | bytes 294916
  106.2 11.4 %copy-start.5 = (bf16[16,48,768]{2,1,0:T(8,128)(2,1)S(1)}, bf16[16,48,768]{2,1,0:T(8,128)(2,1)}, u32[]{:S(2)}) copy-start(bf16[16,48,768]{2,1,0:T(8,128)(2,1)} %get-tuple-element.9) | copy-start | bytes 3538948
  106.7 14.6 %collective-permute-start.16 = (f32[64,768]{1,0:T(8,128)S(1)}, f32[64,768]{1,0:T(8,128)}, u32[]{:S(2)}, u32[]{:S(2)}) collective-permute-start(f32[64,768]{1,0:T(8,128)S(1)} %convolution_bitcast_fusion), channel_id=1, source_target_pairs={{0,16},{16,0},{1,17},{17,1},{2,18},{18,2},{3,19},{19,3},{4,20},{20... | collective-permute-start | bytes 589832 | tf_op jit(solution)/shard_map/ppermute | solution.py:210
  126.4 1.8 collective-permute-start.17
  177.5 1.7 collective-permute-start.18
  183.1 7.2 %collective-permute-start.20 = (f32[64,768]{1,0:T(8,128)S(1)}, f32[64,768]{1,0:T(8,128)S(1)}, u32[]{:S(2)}, u32[]{:S(2)}) collective-permute-start(f32[64,768]{1,0:T(8,128)S(1)} %fusion), channel_id=1, source_target_pairs={{0,16},{16,0},{1,17},{17,1},{2,18},{18,2},{3,19},{19,3},{4,20},{20... | collective-permute-start | bytes 589832 | tf_op jit(solution)/shard_map/ppermute | solution.py:230
  191.5 14.2 %all-to-all-start.7 = ((f32[16,8,384]{2,1,0:T(8,128)}), f32[16,8,384]{2,1,0:T(8,128)S(1)}, u32[]{:S(2)}, u32[]{:S(2)}) async-start(f32[16,8,384]{2,1,0:T(8,128)} %maximum_bitcast_fusion.1), calls=%async_computation.7 | async-start | bytes 393216 | tf_op jit(solution)/shard_map/all_to_all | solution.py:144
  196.0 14.9 %collective-permute-start.19 = (f32[64,64]{1,0:T(8,128)S(1)}, f32[64,64]{1,0:T(8,128)S(1)}, u32[]{:S(2)}, u32[]{:S(2)}) collective-permute-start(f32[64,64]{1,0:T(8,128)S(1)} %fusion.68), channel_id=1, source_target_pairs={{0,16},{16,0},{1,17},{17,1},{2,18},{18,2},{3,19},{19,3},{4,20},{20... | collective-permute-start | bytes 49160 | tf_op jit(solution)/shard_map/ppermute | solution.py:235
  206.4 14.3 %all-to-all-start.8 = ((f32[16,8,384]{2,1,0:T(8,128)}), f32[16,8,384]{2,1,0:T(8,128)S(1)}, u32[]{:S(2)}, u32[]{:S(2)}) async-start(f32[16,8,384]{2,1,0:T(8,128)} %broadcast_in_dim.17), calls=%async_computation.8 | async-start | bytes 393216 | tf_op jit(solution)/shard_map/all_to_all | solution.py:144
  218.5 2.2 copy-start.10
Sparse Core Ops, SparseCore 0:
  10.7 69.8 all-gather.2
